TPU v7x, 32 devices: a whole 2x2x4 slice. The times are simulated.
32 devices in a mesh: pair: 16 (over z, y, x), virt: 2 (over core).
Axes of the slice: x: 2, y: 2, z: 4, core: 2. Of those that a mesh axis runs over, the one named last changes fastest.
Arguments:
- t2_amplitudes: float32 [64, 2048], P('pair', 'virt'), may hold values from -6 to 6
- integral_tiles: float32 [16, 2, 32, 128, 128], P('pair', 'virt'), may hold values from -0.125 to 0.125
- out_tiles: int32 [16, 2, 32], P('pair', 'virt'), may hold values from 0 to 15, as said below
- in_tiles: int32 [16, 2, 32], P('pair', 'virt'), may hold values from 0 to 15
- tile_counts: int32 [16, 2], P('pair', 'virt'), may hold values from 1 to 32, as said below
Outputs:
- ladder: float32 [64, 2048], P('pair', 'virt')
Inputs may be any that keep to these rules, and one draw needn't show every extreme that they name: `out_tiles`: slots of the devices at virt index v name output tiles v * 8 to (v + 1) * 8 - 1 only. `tile_counts`: in every draw some device has all 32 slots live.
All inputs are finite; a program needn't handle non-finite values.
Results may differ from a plain program's by a relative error of at most 0.0003.
Values sent between devices are 32-bit elements; how exact they have to be, the bound alone decides.
No kernel may reach another device: no remote copies, remote signals or barrier semaphores. Data moves between devices by JAX's collectives and lax.ppermute only.
A program may use at most 64 MiB of HBM per device.

v0:
```python
import jax
import jax.numpy as jnp
from jax import lax
from jax.experimental import pallas as pl
from jax.experimental.pallas import tpu as pltpu
from jax.sharding import PartitionSpec as P

W = 128
GROUP = 8
NEAR = 4
SMEM = pl.BlockSpec(memory_space=pltpu.SMEM)
VMEM = pl.BlockSpec(memory_space=pltpu.VMEM)


def split(value):
    high = value.astype(jnp.bfloat16)
    low = (value - high.astype(jnp.float32)).astype(jnp.bfloat16)
    return high, low


def tile_kernel(out_tiles, live, ins, outs, tiles, mine, halves, codes, own, held, index_rows, arrived, singles):
    singles_of = ((ins, index_rows.at[0]), (outs, index_rows.at[1]), (mine, own))
    others = [pltpu.make_async_copy(here, there, singles.at[at]) for at, (here, there) in enumerate(singles_of)]
    for copy in others:
        copy.start()
    count = live[0, 0]
    groups = (count + GROUP - 1) // GROUP

    def tile_copy(index):
        part = pl.ds(index * GROUP, GROUP)
        return pltpu.make_async_copy(tiles.at[part], held.at[part], arrived.at[index])

    def begin(index, carry):
        tile_copy(index).start()
        return carry

    lax.fori_loop(0, groups, begin, 0)
    for copy in others:
        copy.wait()
    slots = lax.broadcasted_iota(jnp.int32, ins.shape, 1)
    tile_in = index_rows[0]
    owner = lax.bitwise_xor(lax.div(tile_in, out_tiles), lax.axis_index("virt"))
    codes[0:1, :] = owner * out_tiles + lax.rem(tile_in, out_tiles)
    codes[1:2, :] = jnp.where(slots < count, lax.rem(index_rows[1], out_tiles), out_tiles)
    codes[2:3, :] = jnp.full(ins.shape, count, jnp.int32)

    def one_group(index, carry):
        tile_copy(index).wait()
        for step in range(GROUP):
            slot = index * GROUP + step
            high, low = split(held[slot])
            halves[slot, :, :W] = high
            halves[slot, :, W:] = low
        return carry

    lax.fori_loop(0, groups, one_group, 0)


def prepare(tiles, ins, outs, live, mine, out_tiles):
    slots = tiles.shape[0]

    def kernel(*refs):
        tile_kernel(out_tiles, *refs)

    operands = [pltpu.with_memory_space_constraint(value, pltpu.HBM) for value in (ins, outs, tiles, mine)]
    return pl.pallas_call(
        kernel,
        out_shape=(
            jax.ShapeDtypeStruct((slots, W, 2 * W), jnp.bfloat16),
            jax.ShapeDtypeStruct((3, slots), jnp.int32),
            jax.ShapeDtypeStruct(mine.shape, mine.dtype),
        ),
        in_specs=[SMEM] + [pl.BlockSpec(memory_space=pltpu.HBM)] * 4,
        out_specs=(VMEM, VMEM, VMEM),
        scratch_shapes=[
            pltpu.VMEM((slots, W, W), jnp.float32),
            pltpu.VMEM((2, 1, slots), jnp.int32),
            pltpu.SemaphoreType.DMA((slots // GROUP,)),
            pltpu.SemaphoreType.DMA((3,)),
        ],
        compiler_params=pltpu.CompilerParams(vmem_limit_bytes=32 * 1024 * 1024),
        cost_estimate=pl.CostEstimate(flops=4 * slots * W * W, bytes_accessed=8 * slots * W * W, transcendentals=0),
    )(live, *operands)


def ladder_kernel(virts, codes, halves, *refs):
    blocks, (result, columns, flat, totals) = refs[: virts * NEAR], refs[virts * NEAR :]
    far = blocks[0].shape[0]
    chunk_count = NEAR * far
    out_tiles = totals.shape[0] - 1
    rows = result.shape[1] // out_tiles
    in_local = columns.shape[0] // virts
    totals[...] = jnp.zeros_like(totals)

    for owner in range(virts):
        for a in range(NEAR):
            for b in range(far):
                source = blocks[(owner ^ int((a > 0) != (b > 0))) * NEAR + a]
                place = pl.ds((a * far + b) * rows, rows)
                for tile in range(in_local):
                    flat[tile, place, :] = source[b, tile * rows : (tile + 1) * rows, :]
        for tile in range(in_local):
            high, low = split(flat[tile])
            columns[owner * in_local + tile, :, :W] = high
            columns[owner * in_local + tile, :, W:] = low

    def one_group(index, carry):
        first = index * GROUP
        products = []
        for step in range(GROUP):
            both = halves[first + step]
            weights = jnp.concatenate([both, both], axis=0)
            got = jnp.dot(columns[codes[0, first + step]], weights, preferred_element_type=jnp.float32)
            products.append(got[:, :W] + got[:, W:])
        for step in range(GROUP):
            place = codes[1, first + step]
            totals[place] = totals[place] + products[step]
        return carry

    lax.fori_loop(0, (codes[2, 0] + GROUP - 1) // GROUP, one_group, 0)
    me = lax.axis_index("pair")

    def give(chunk, carry):
        device = lax.bitwise_xor(me, lax.rem(chunk, far) * NEAR + chunk // far)
        for tile in range(out_tiles):
            result[device, tile * rows : (tile + 1) * rows, :] = totals[tile, pl.ds(chunk * rows, rows), :]
        return carry

    lax.fori_loop(0, chunk_count, give, 0, unroll=min(chunk_count, 16))


def local_terms(codes, blocks, halves, rows, out_tiles):
    far, chunk_rows, _ = blocks[0].shape
    virts = len(blocks) // NEAR
    total_rows = NEAR * far * rows
    in_local = chunk_rows // rows

    def kernel(*refs):
        ladder_kernel(virts, *refs)

    return pl.pallas_call(
        kernel,
        out_shape=jax.ShapeDtypeStruct((NEAR * far, out_tiles * rows, W), jnp.float32),
        in_specs=[SMEM, VMEM] + [VMEM] * len(blocks),
        out_specs=VMEM,
        scratch_shapes=[
            pltpu.VMEM((virts * in_local, total_rows, 2 * W), jnp.bfloat16),
            pltpu.VMEM((in_local, total_rows, W), jnp.float32),
            pltpu.VMEM((out_tiles + 1, total_rows, W), jnp.float32),
        ],
        compiler_params=pltpu.CompilerParams(vmem_limit_bytes=32 * 1024 * 1024),
    )(codes, halves, *blocks)


def swap(value, pairs, virts, mask, virt_mask):
    routes = [(a * virts + b, (a ^ mask) * virts + (b ^ virt_mask)) for a in range(pairs) for b in range(virts)]
    return lax.ppermute(value, ("pair", "virt"), routes)


def shards(t2_amplitudes, integral_tiles, out_tiles, in_tiles, tile_counts):
    rows, columns = t2_amplitudes.shape
    local_tiles = columns // W
    slots = integral_tiles.shape[2]
    pairs, virts = lax.axis_size("pair"), lax.axis_size("virt")
    mine = t2_amplitudes.reshape(rows, local_tiles, W).transpose(1, 0, 2).reshape(local_tiles * rows, W)
    halves, codes, own = prepare(
        integral_tiles.reshape(slots, W, W),
        in_tiles.reshape(1, slots),
        out_tiles.reshape(1, slots),
        tile_counts,
        mine,
        local_tiles,
    )
    line = jnp.stack([own] + [swap(mine, pairs, virts, mask, 1) for mask in range(NEAR, pairs, NEAR)])
    pieces = [line] + [swap(line, pairs, virts, mask, 1) for mask in range(1, NEAR)]
    blocks = pieces + [swap(piece, pairs, virts, 0, mask) for mask in range(1, virts) for piece in pieces]
    partial_sums = local_terms(codes, blocks, halves, rows, local_tiles)
    received = lax.all_to_all(partial_sums, "pair", 0, 0)
    summed = jnp.sum(received, axis=0)
    return summed.reshape(local_tiles, rows, W).transpose(1, 0, 2).reshape(rows, columns)


def solution(mesh):
    return jax.shard_map(
        shards,
        mesh=mesh,
        in_specs=(
            P("pair", "virt"),
            P("pair", "virt", None, None, None),
            P("pair", "virt", None),
            P("pair", "virt", None),
            P("pair", "virt"),
        ),
        out_specs=P("pair", "virt"),
        check_vma=False,
    )
```

profile of v0, /device:TPU:0, one launch (start us, length us, event | category | flops | bytes accessed | tf_op | source)
XLA Modules:
  0.0 34.5 jit_solution(15657430246091368455)
XLA Ops:
  0.0 4.5 %collective-permute-start.2 = (f32[32,128]{1,0:T(8,128)}, f32[32,128]{1,0:T(8,128)S(1)}, u32[]{:S(2)}, u32[]{:S(2)}) collective-permute-start(f32[32,128]{1,0:T(8,128)} %bitcast.19), channel_id=1, source_target_pairs={{0,25},{1,24},{2,27},{3,26},{4,29},{5,28},{6,31},{7,30},{8,17},{9,... | collective-permute-start | bytes 49160 | tf_op jit(solution)/shard_map/ppermute | solution.py:157
  4.5 0.0 collective-permute-start.1
  4.5 0.8 %collective-permute-start = (f32[32,128]{1,0:T(8,128)}, f32[32,128]{1,0:T(8,128)S(1)}, u32[]{:S(2)}, u32[]{:S(2)}) collective-permute-start(f32[32,128]{1,0:T(8,128)} %bitcast.21), channel_id=1, source_target_pairs={{0,9},{1,8},{2,11},{3,10},{4,13},{5,12},{6,15},{7,14},{8,1},{9,0},... | collective-permute-start | bytes 49160 | tf_op jit(solution)/shard_map/ppermute | solution.py:157
  6.0 1.2 %shard_map.55 = (bf16[32,128,256]{2,1,0:T(8,128)(2,1)S(1)}, s32[3,32]{1,0:T(4,128)S(1)}, f32[32,128]{1,0:T(8,128)S(1)}) custom-call(s32[1,1]{1,0:T(1,128)S(6)} %copy.8.refs_0_, s32[1,32]{1,0:T(1,128)} %bitcast.26, s32[1,32]{1,0:T(1,128)} %bitcast.27, f32[32,128,128]{2,1,0:T(8,128)} %bitcast.18, f32[32,128]{1,0:T(8,128)} %bitcast.22), custom_call_target="tpu_custom_call" | custom-call | flops 2097152 | bytes 4194304 | tf_op jit(solution)/shard_map/pallas_call | solution.py:66
  7.2 0.0 collective-permute-done.2
  7.2 1.6 %collective-permute-done.1 = f32[32,128]{1,0:T(8,128)S(1)} collective-permute-done((f32[32,128]{1,0:T(8,128)}, f32[32,128]{1,0:T(8,128)S(1)}, u32[]{:S(2)}, u32[]{:S(2)}) %collective-permute-start.1) | collective-permute-done | bytes 16416 | tf_op jit(solution)/shard_map/ppermute | solution.py:157
  8.9 0.0 collective-permute-done
  8.9 2.7 %collective-permute-start.5 = (f32[4,32,128]{2,1,0:T(8,128)S(1)}, f32[4,32,128]{2,1,0:T(8,128)S(1)}, u32[]{:S(2)}, u32[]{:S(2)}) collective-permute-start(f32[4,32,128]{2,1,0:T(8,128)S(1)} %pad_maximum_fusion.refs_2_), channel_id=1, source_target_pairs={{0,7},{1,6},{2,5},{3,4},{4,3},{5,2},{6,1},{7,0},{8,15},{9,14},{10,... | collective-permute-start | bytes 196616 | tf_op jit(solution)/shard_map/ppermute | solution.py:157
  11.6 0.1 collective-permute-start.4
  11.6 0.7 %collective-permute-start.3 = (f32[4,32,128]{2,1,0:T(8,128)S(1)}, f32[4,32,128]{2,1,0:T(8,128)S(1)}, u32[]{:S(2)}, u32[]{:S(2)}) collective-permute-start(f32[4,32,128]{2,1,0:T(8,128)S(1)} %pad_maximum_fusion.refs_2_), channel_id=1, source_target_pairs={{0,3},{1,2},{2,1},{3,0},{4,7},{5,6},{6,5},{7,4},{8,11},{9,10},{10,... | collective-permute-start | bytes 196616 | tf_op jit(solution)/shard_map/ppermute | solution.py:157
  12.3 0.0 collective-permute-start.6
  12.3 1.6 %collective-permute-done.5.refs_5_ = f32[4,32,128]{2,1,0:T(8,128)S(1)} collective-permute-done((f32[4,32,128]{2,1,0:T(8,128)S(1)}, f32[4,32,128]{2,1,0:T(8,128)S(1)}, u32[]{:S(2)}, u32[]{:S(2)}) %collective-permute-start.5) | collective-permute-done | bytes 65568 | tf_op jit(solution)/shard_map/ppermute | solution.py:157
  14.0 0.1 collective-permute-start.9
  14.1 1.7 %collective-permute-done.4.refs_4_ = f32[4,32,128]{2,1,0:T(8,128)S(1)} collective-permute-done((f32[4,32,128]{2,1,0:T(8,128)S(1)}, f32[4,32,128]{2,1,0:T(8,128)S(1)}, u32[]{:S(2)}, u32[]{:S(2)}) %collective-permute-start.4) | collective-permute-done | bytes 65568 | tf_op jit(solution)/shard_map/ppermute | solution.py:157
  15.8 0.1 collective-permute-start.8
  15.9 0.0 collective-permute-done.3.refs_3_
  15.9 0.4 %collective-permute-start.7 = (f32[4,32,128]{2,1,0:T(8,128)S(1)}, f32[4,32,128]{2,1,0:T(8,128)S(1)}, u32[]{:S(2)}, u32[]{:S(2)}) collective-permute-start(f32[4,32,128]{2,1,0:T(8,128)S(1)} %collective-permute-done.3.refs_3_), channel_id=1, source_target_pairs={{0,1},{1,0},{2,3},{3,2},{4,5},{5,4},{6,7},{7,6},{8,9},{9,8},{10,11... | collective-permute-start | bytes 196616 | tf_op jit(solution)/shard_map/ppermute | solution.py:157
  16.3 0.0 collective-permute-done.6.refs_6_
  16.3 0.0 collective-permute-done.9.refs_9_
  16.3 0.7 %collective-permute-done.8.refs_8_ = f32[4,32,128]{2,1,0:T(8,128)S(1)} collective-permute-done((f32[4,32,128]{2,1,0:T(8,128)S(1)}, f32[4,32,128]{2,1,0:T(8,128)S(1)}, u32[]{:S(2)}, u32[]{:S(2)}) %collective-permute-start.8) | collective-permute-done | bytes 65568 | tf_op jit(solution)/shard_map/ppermute | solution.py:157
  17.1 0.2 collective-permute-done.7.refs_7_
  17.2 1.1 %shard_map.56 = f32[16,32,128]{2,1,0:T(8,128)S(1)} custom-call(s32[3,32]{1,0:T(4,128)S(1)} %get-tuple-element.8.refs_0_, bf16[32,128,256]{2,1,0:T(8,128)(2,1)S(1)} %get-tuple-element.9.refs_1_, f32[4,32,128]{2,1,0:T(8,128)S(1)} %pad_maximum_fusion.refs_2_, f32[4,32,128]{2,1,0:T(8,128)S(1)} %collective-permute-done.3.refs_3_, ...), custom_call_target="tpu_custom_call" | custom-call | tf_op jit(solution)/shard_map/pallas_call | solution.py:141
  18.3 15.5 %all_to_all.5 = f32[16,32,128]{2,1,0:T(8,128)S(1)} all-to-all(f32[16,32,128]{2,1,0:T(8,128)S(1)} %shard_map.56), channel_id=1, replica_groups=mesh['pair'=16,'virt'=2] {'pair'}, dimensions={0} | all-to-all | bytes 524288 | tf_op jit(solution)/shard_map/all_to_all | solution.py:178
  33.9 0.6 %reduce_sum.9 = f32[32,128]{1,0:T(8,128)} reduce(f32[16,32,128]{2,1,0:T(8,128)S(1)} %all_to_all.5, f32[]{:T(128)} %constant.0.clone.1), dimensions={0}, to_apply=%region_0.0 | reduce | flops 61440 | bytes 278532 | tf_op jit(solution)/shard_map/reduce_sum | solution.py:179
  (1 shorter events, 0.0 us)
Async XLA Ops:
  0.0 7.2 %collective-permute-start.2 = (f32[32,128]{1,0:T(8,128)}, f32[32,128]{1,0:T(8,128)S(1)}, u32[]{:S(2)}, u32[]{:S(2)}) collective-permute-start(f32[32,128]{1,0:T(8,128)} %bitcast.19), channel_id=1, source_target_pairs={{0,25},{1,24},{2,27},{3,26},{4,29},{5,28},{6,31},{7,30},{8,17},{9,... | collective-permute-start | bytes 49160 | tf_op jit(solution)/shard_map/ppermute | solution.py:157
  4.5 4.4 %collective-permute-start.1 = (f32[32,128]{1,0:T(8,128)}, f32[32,128]{1,0:T(8,128)S(1)}, u32[]{:S(2)}, u32[]{:S(2)}) collective-permute-start(f32[32,128]{1,0:T(8,128)} %bitcast.20), channel_id=1, source_target_pairs={{0,17},{1,16},{2,19},{3,18},{4,21},{5,20},{6,23},{7,22},{8,25},{9,... | collective-permute-start | bytes 49160 | tf_op jit(solution)/shard_map/ppermute | solution.py:157
  4.5 4.4 %collective-permute-start = (f32[32,128]{1,0:T(8,128)}, f32[32,128]{1,0:T(8,128)S(1)}, u32[]{:S(2)}, u32[]{:S(2)}) collective-permute-start(f32[32,128]{1,0:T(8,128)} %bitcast.21), channel_id=1, source_target_pairs={{0,9},{1,8},{2,11},{3,10},{4,13},{5,12},{6,15},{7,14},{8,1},{9,0},... | collective-permute-start | bytes 49160 | tf_op jit(solution)/shard_map/ppermute | solution.py:157
  8.9 5.1 %collective-permute-start.5 = (f32[4,32,128]{2,1,0:T(8,128)S(1)}, f32[4,32,128]{2,1,0:T(8,128)S(1)}, u32[]{:S(2)}, u32[]{:S(2)}) collective-permute-start(f32[4,32,128]{2,1,0:T(8,128)S(1)} %pad_maximum_fusion.refs_2_), channel_id=1, source_target_pairs={{0,7},{1,6},{2,5},{3,4},{4,3},{5,2},{6,1},{7,0},{8,15},{9,14},{10,... | collective-permute-start | bytes 196616 | tf_op jit(solution)/shard_map/ppermute | solution.py:157
  11.6 4.3 %collective-permute-start.4 = (f32[4,32,128]{2,1,0:T(8,128)S(1)}, f32[4,32,128]{2,1,0:T(8,128)S(1)}, u32[]{:S(2)}, u32[]{:S(2)}) collective-permute-start(f32[4,32,128]{2,1,0:T(8,128)S(1)} %pad_maximum_fusion.refs_2_), channel_id=1, source_target_pairs={{0,5},{1,4},{2,7},{3,6},{4,1},{5,0},{6,3},{7,2},{8,13},{9,12},{10,... | collective-permute-start | bytes 196616 | tf_op jit(solution)/shard_map/ppermute | solution.py:157
  11.6 4.3 %collective-permute-start.3 = (f32[4,32,128]{2,1,0:T(8,128)S(1)}, f32[4,32,128]{2,1,0:T(8,128)S(1)}, u32[]{:S(2)}, u32[]{:S(2)}) collective-permute-start(f32[4,32,128]{2,1,0:T(8,128)S(1)} %pad_maximum_fusion.refs_2_), channel_id=1, source_target_pairs={{0,3},{1,2},{2,1},{3,0},{4,7},{5,6},{6,5},{7,4},{8,11},{9,10},{10,... | collective-permute-start | bytes 196616 | tf_op jit(solution)/shard_map/ppermute | solution.py:157
  12.3 4.0 %collective-permute-start.6 = (f32[4,32,128]{2,1,0:T(8,128)S(1)}, f32[4,32,128]{2,1,0:T(8,128)S(1)}, u32[]{:S(2)}, u32[]{:S(2)}) collective-permute-start(f32[4,32,128]{2,1,0:T(8,128)S(1)} %pad_maximum_fusion.refs_2_), channel_id=1, source_target_pairs={{0,1},{1,0},{2,3},{3,2},{4,5},{5,4},{6,7},{7,6},{8,9},{9,8},{10,11... | collective-permute-start | bytes 196616 | tf_op jit(solution)/shard_map/ppermute | solution.py:157
  14.0 2.4 %collective-permute-start.9 = (f32[4,32,128]{2,1,0:T(8,128)S(1)}, f32[4,32,128]{2,1,0:T(8,128)S(1)}, u32[]{:S(2)}, u32[]{:S(2)}) collective-permute-start(f32[4,32,128]{2,1,0:T(8,128)S(1)} %collective-permute-done.5.refs_5_), channel_id=1, source_target_pairs={{0,1},{1,0},{2,3},{3,2},{4,5},{5,4},{6,7},{7,6},{8,9},{9,8},{10,11... | collective-permute-start | bytes 196616 | tf_op jit(solution)/shard_map/ppermute | solution.py:157
  15.8 1.3 %collective-permute-start.8 = (f32[4,32,128]{2,1,0:T(8,128)S(1)}, f32[4,32,128]{2,1,0:T(8,128)S(1)}, u32[]{:S(2)}, u32[]{:S(2)}) collective-permute-start(f32[4,32,128]{2,1,0:T(8,128)S(1)} %collective-permute-done.4.refs_4_), channel_id=1, source_target_pairs={{0,1},{1,0},{2,3},{3,2},{4,5},{5,4},{6,7},{7,6},{8,9},{9,8},{10,11... | collective-permute-start | bytes 196616 | tf_op jit(solution)/shard_map/ppermute | solution.py:157
  15.9 1.3 %collective-permute-start.7 = (f32[4,32,128]{2,1,0:T(8,128)S(1)}, f32[4,32,128]{2,1,0:T(8,128)S(1)}, u32[]{:S(2)}, u32[]{:S(2)}) collective-permute-start(f32[4,32,128]{2,1,0:T(8,128)S(1)} %collective-permute-done.3.refs_3_), channel_id=1, source_target_pairs={{0,1},{1,0},{2,3},{3,2},{4,5},{5,4},{6,7},{7,6},{8,9},{9,8},{10,11... | collective-permute-start | bytes 196616 | tf_op jit(solution)/shard_map/ppermute | solution.py:157
where the time goes:
time: 34.6 us; the launch traced here: 34.5 us
  blocking collectives  15.5 us (45%)
  starting transfers between devices  9.4 us (27%)
  waiting for transfers between devices  5.91 us (17%)
  Pallas kernels  2.33 us (7%)
  between operations  0.69 us (2%)
  other arithmetic  0.63 us (2%)
    all_to_all x1, blocking collectives, shards(): received = lax.all_to_all(partial_sums, 'pair', 0, 0)  15.5 us
    ppermute x10, starting transfers between devices, swap(): return lax.ppermute(value, ('pair', 'virt'), routes)  9.4 us
    ppermute x10, waiting for transfers between devices, swap(): return lax.ppermute(value, ('pair', 'virt'), routes)  5.91 us
    pallas_call x1, Pallas kernels, prepare(): pl.pallas_call(kernel, out_shape=(jax.ShapeDtypeStruct((slots, W, 2 * W),...  1.24 us
    pallas_call x1, Pallas kernels, local_terms(): pl.pallas_call(kernel, out_shape=jax.ShapeDtypeStruct((NEAR * far, out_ti...  1.09 us
  transfers between devices with their start and end apart: 10, of which 5 were waited for; matrix products, arithmetic and copies ran while one was open for 0% of the time, Pallas kernels for 4%

commit v1 on v0

--- a/solution.py
+++ b/solution.py
@@ -83,12 +83,15 @@
     )(live, *operands)
 
 
-def ladder_kernel(virts, codes, halves, *refs):
-    blocks, (result, columns, flat, totals) = refs[: virts * NEAR], refs[virts * NEAR :]
+def ladder_kernel(virts, codes_here, halves, *refs):
+    blocks, (result, columns, flat, totals, codes, copied) = refs[: virts * NEAR], refs[virts * NEAR :]
+    fetch = pltpu.make_async_copy(codes_here, codes, copied)
+    fetch.start()
     far = blocks[0].shape[0]
     chunk_count = NEAR * far
     out_tiles = totals.shape[0] - 1
     rows = result.shape[1] // out_tiles
+    total_rows = chunk_count * rows
     in_local = columns.shape[0] // virts
     totals[...] = jnp.zeros_like(totals)
 
@@ -101,17 +104,19 @@
                     flat[tile, place, :] = source[b, tile * rows : (tile + 1) * rows, :]
         for tile in range(in_local):
             high, low = split(flat[tile])
-            columns[owner * in_local + tile, :, :W] = high
-            columns[owner * in_local + tile, :, W:] = low
+            columns[owner * in_local + tile, :total_rows, :] = high
+            columns[owner * in_local + tile, total_rows:, :] = low
+
+    fetch.wait()
 
     def one_group(index, carry):
         first = index * GROUP
         products = []
         for step in range(GROUP):
-            both = halves[first + step]
-            weights = jnp.concatenate([both, both], axis=0)
-            got = jnp.dot(columns[codes[0, first + step]], weights, preferred_element_type=jnp.float32)
-            products.append(got[:, :W] + got[:, W:])
+            both = columns[codes[0, first + step]]
+            upper = jnp.dot(both, halves[first + step, :, :W], preferred_element_type=jnp.float32)
+            lower = jnp.dot(both[:total_rows], halves[first + step, :, W:], preferred_element_type=jnp.float32)
+            products.append(upper[:total_rows] + (upper[total_rows:] + lower))
         for step in range(GROUP):
             place = codes[1, first + step]
             totals[place] = totals[place] + products[step]
@@ -141,12 +146,14 @@
     return pl.pallas_call(
         kernel,
         out_shape=jax.ShapeDtypeStruct((NEAR * far, out_tiles * rows, W), jnp.float32),
-        in_specs=[SMEM, VMEM] + [VMEM] * len(blocks),
+        in_specs=[VMEM, VMEM] + [VMEM] * len(blocks),
         out_specs=VMEM,
         scratch_shapes=[
-            pltpu.VMEM((virts * in_local, total_rows, 2 * W), jnp.bfloat16),
+            pltpu.VMEM((virts * in_local, 2 * total_rows, W), jnp.bfloat16),
             pltpu.VMEM((in_local, total_rows, W), jnp.float32),
             pltpu.VMEM((out_tiles + 1, total_rows, W), jnp.float32),
+            pltpu.SMEM(codes.shape, jnp.int32),
+            pltpu.SemaphoreType.DMA,
         ],
         compiler_params=pltpu.CompilerParams(vmem_limit_bytes=32 * 1024 * 1024),
     )(codes, halves, *blocks)

time: 34.6 us -> 33.9 us (0.980)
  blocking collectives: 15.5 us -> 15 us
    all_to_all x1, blocking collectives: 15.5 us -> 15 us  [shards(): received = lax.all_to_all(partial_sums, 'pair', 0, 0)]
where the time goes in v1:
time: 33.9 us; the launch traced here: 33.8 us
  blocking collectives  15 us (44%)
  starting transfers between devices  9.4 us (28%)
  waiting for transfers between devices  5.91 us (17%)
  Pallas kernels  2.17 us (6%)
  between operations  0.69 us (2%)
  other arithmetic  0.63 us (2%)
    all_to_all x1, blocking collectives, shards(): received = lax.all_to_all(partial_sums, 'pair', 0, 0)  15 us
    ppermute x10, starting transfers between devices, swap(): return lax.ppermute(value, ('pair', 'virt'), routes)  9.4 us
    ppermute x10, waiting for transfers between devices, swap(): return lax.ppermute(value, ('pair', 'virt'), routes)  5.91 us
    pallas_call x1, Pallas kernels, prepare(): pl.pallas_call(kernel, out_shape=(jax.ShapeDtypeStruct((slots, W, 2 * W),...  1.24 us
    pallas_call x1, Pallas kernels, local_terms(): pl.pallas_call(kernel, out_shape=jax.ShapeDtypeStruct((NEAR * far, out_ti...  0.93 us
  transfers between devices with their start and end apart: 10, of which 5 were waited for; matrix products, arithmetic and copies ran while one was open for 0% of the time, Pallas kernels for 4%

profile of v1, /device:TPU:0, one launch (start us, length us, event | category | flops | bytes accessed | tf_op | source)
XLA Modules:
  0.0 33.8 jit_solution(1839889778145816578)
XLA Ops:
  0.0 4.5 %collective-permute-start.2 = (f32[32,128]{1,0:T(8,128)}, f32[32,128]{1,0:T(8,128)S(1)}, u32[]{:S(2)}, u32[]{:S(2)}) collective-permute-start(f32[32,128]{1,0:T(8,128)} %bitcast.19), channel_id=1, source_target_pairs={{0,25},{1,24},{2,27},{3,26},{4,29},{5,28},{6,31},{7,30},{8,17},{9,... | collective-permute-start | bytes 49160 | tf_op jit(solution)/shard_map/ppermute | solution.py:164
  4.5 0.0 collective-permute-start.1
  4.5 0.8 %collective-permute-start = (f32[32,128]{1,0:T(8,128)}, f32[32,128]{1,0:T(8,128)S(1)}, u32[]{:S(2)}, u32[]{:S(2)}) collective-permute-start(f32[32,128]{1,0:T(8,128)} %bitcast.21), channel_id=1, source_target_pairs={{0,9},{1,8},{2,11},{3,10},{4,13},{5,12},{6,15},{7,14},{8,1},{9,0},... | collective-permute-start | bytes 49160 | tf_op jit(solution)/shard_map/ppermute | solution.py:164
  6.0 1.2 %shard_map.55 = (bf16[32,128,256]{2,1,0:T(8,128)(2,1)S(1)}, s32[3,32]{1,0:T(4,128)S(1)}, f32[32,128]{1,0:T(8,128)S(1)}) custom-call(s32[1,1]{1,0:T(1,128)S(6)} %copy.8.refs_0_, s32[1,32]{1,0:T(1,128)} %bitcast.26, s32[1,32]{1,0:T(1,128)} %bitcast.27, f32[32,128,128]{2,1,0:T(8,128)} %bitcast.18, f32[32,128]{1,0:T(8,128)} %bitcast.22), custom_call_target="tpu_custom_call" | custom-call | flops 2097152 | bytes 4194304 | tf_op jit(solution)/shard_map/pallas_call | solution.py:66
  7.2 0.0 collective-permute-done.2
  7.2 1.6 %collective-permute-done.1 = f32[32,128]{1,0:T(8,128)S(1)} collective-permute-done((f32[32,128]{1,0:T(8,128)}, f32[32,128]{1,0:T(8,128)S(1)}, u32[]{:S(2)}, u32[]{:S(2)}) %collective-permute-start.1) | collective-permute-done | bytes 16416 | tf_op jit(solution)/shard_map/ppermute | solution.py:164
  8.9 0.0 collective-permute-done
  8.9 2.7 %collective-permute-start.5 = (f32[4,32,128]{2,1,0:T(8,128)S(1)}, f32[4,32,128]{2,1,0:T(8,128)S(1)}, u32[]{:S(2)}, u32[]{:S(2)}) collective-permute-start(f32[4,32,128]{2,1,0:T(8,128)S(1)} %pad_maximum_fusion.refs_2_), channel_id=1, source_target_pairs={{0,7},{1,6},{2,5},{3,4},{4,3},{5,2},{6,1},{7,0},{8,15},{9,14},{10,... | collective-permute-start | bytes 196616 | tf_op jit(solution)/shard_map/ppermute | solution.py:164
  11.6 0.1 collective-permute-start.4
  11.6 0.7 %collective-permute-start.3 = (f32[4,32,128]{2,1,0:T(8,128)S(1)}, f32[4,32,128]{2,1,0:T(8,128)S(1)}, u32[]{:S(2)}, u32[]{:S(2)}) collective-permute-start(f32[4,32,128]{2,1,0:T(8,128)S(1)} %pad_maximum_fusion.refs_2_), channel_id=1, source_target_pairs={{0,3},{1,2},{2,1},{3,0},{4,7},{5,6},{6,5},{7,4},{8,11},{9,10},{10,... | collective-permute-start | bytes 196616 | tf_op jit(solution)/shard_map/ppermute | solution.py:164
  12.3 0.0 collective-permute-start.6
  12.3 1.6 %collective-permute-done.5.refs_5_ = f32[4,32,128]{2,1,0:T(8,128)S(1)} collective-permute-done((f32[4,32,128]{2,1,0:T(8,128)S(1)}, f32[4,32,128]{2,1,0:T(8,128)S(1)}, u32[]{:S(2)}, u32[]{:S(2)}) %collective-permute-start.5) | collective-permute-done | bytes 65568 | tf_op jit(solution)/shard_map/ppermute | solution.py:164
  14.0 0.1 collective-permute-start.9
  14.1 1.7 %collective-permute-done.4.refs_4_ = f32[4,32,128]{2,1,0:T(8,128)S(1)} collective-permute-done((f32[4,32,128]{2,1,0:T(8,128)S(1)}, f32[4,32,128]{2,1,0:T(8,128)S(1)}, u32[]{:S(2)}, u32[]{:S(2)}) %collective-permute-start.4) | collective-permute-done | bytes 65568 | tf_op jit(solution)/shard_map/ppermute | solution.py:164
  15.8 0.1 collective-permute-start.8
  15.9 0.0 collective-permute-done.3.refs_3_
  15.9 0.4 %collective-permute-start.7 = (f32[4,32,128]{2,1,0:T(8,128)S(1)}, f32[4,32,128]{2,1,0:T(8,128)S(1)}, u32[]{:S(2)}, u32[]{:S(2)}) collective-permute-start(f32[4,32,128]{2,1,0:T(8,128)S(1)} %collective-permute-done.3.refs_3_), channel_id=1, source_target_pairs={{0,1},{1,0},{2,3},{3,2},{4,5},{5,4},{6,7},{7,6},{8,9},{9,8},{10,11... | collective-permute-start | bytes 196616 | tf_op jit(solution)/shard_map/ppermute | solution.py:164
  16.3 0.0 collective-permute-done.6.refs_6_
  16.3 0.0 collective-permute-done.9.refs_9_
  16.3 0.7 %collective-permute-done.8.refs_8_ = f32[4,32,128]{2,1,0:T(8,128)S(1)} collective-permute-done((f32[4,32,128]{2,1,0:T(8,128)S(1)}, f32[4,32,128]{2,1,0:T(8,128)S(1)}, u32[]{:S(2)}, u32[]{:S(2)}) %collective-permute-start.8) | collective-permute-done | bytes 65568 | tf_op jit(solution)/shard_map/ppermute | solution.py:164
  17.1 0.2 collective-permute-done.7.refs_7_
  17.2 0.9 %shard_map.56 = f32[16,32,128]{2,1,0:T(8,128)S(1)} custom-call(s32[3,32]{1,0:T(4,128)S(1)} %get-tuple-element.8.refs_0_, bf16[32,128,256]{2,1,0:T(8,128)(2,1)S(1)} %get-tuple-element.9.refs_1_, f32[4,32,128]{2,1,0:T(8,128)S(1)} %pad_maximum_fusion.refs_2_, f32[4,32,128]{2,1,0:T(8,128)S(1)} %collective-permute-done.3.refs_3_, ...), custom_call_target="tpu_custom_call" | custom-call | tf_op jit(solution)/shard_map/pallas_call | solution.py:146
  18.2 15.0 %all_to_all.5 = f32[16,32,128]{2,1,0:T(8,128)S(1)} all-to-all(f32[16,32,128]{2,1,0:T(8,128)S(1)} %shard_map.56), channel_id=1, replica_groups=mesh['pair'=16,'virt'=2] {'pair'}, dimensions={0} | all-to-all | bytes 524288 | tf_op jit(solution)/shard_map/all_to_all | solution.py:185
  33.2 0.6 %reduce_sum.9 = f32[32,128]{1,0:T(8,128)} reduce(f32[16,32,128]{2,1,0:T(8,128)S(1)} %all_to_all.5, f32[]{:T(128)} %constant.0.clone.1), dimensions={0}, to_apply=%region_0.0 | reduce | flops 61440 | bytes 278532 | tf_op jit(solution)/shard_map/reduce_sum | solution.py:186
  (1 shorter events, 0.0 us)
Async XLA Ops:
  0.0 7.2 %collective-permute-start.2 = (f32[32,128]{1,0:T(8,128)}, f32[32,128]{1,0:T(8,128)S(1)}, u32[]{:S(2)}, u32[]{:S(2)}) collective-permute-start(f32[32,128]{1,0:T(8,128)} %bitcast.19), channel_id=1, source_target_pairs={{0,25},{1,24},{2,27},{3,26},{4,29},{5,28},{6,31},{7,30},{8,17},{9,... | collective-permute-start | bytes 49160 | tf_op jit(solution)/shard_map/ppermute | solution.py:164
  4.5 4.4 %collective-permute-start.1 = (f32[32,128]{1,0:T(8,128)}, f32[32,128]{1,0:T(8,128)S(1)}, u32[]{:S(2)}, u32[]{:S(2)}) collective-permute-start(f32[32,128]{1,0:T(8,128)} %bitcast.20), channel_id=1, source_target_pairs={{0,17},{1,16},{2,19},{3,18},{4,21},{5,20},{6,23},{7,22},{8,25},{9,... | collective-permute-start | bytes 49160 | tf_op jit(solution)/shard_map/ppermute | solution.py:164
  4.5 4.4 %collective-permute-start = (f32[32,128]{1,0:T(8,128)}, f32[32,128]{1,0:T(8,128)S(1)}, u32[]{:S(2)}, u32[]{:S(2)}) collective-permute-start(f32[32,128]{1,0:T(8,128)} %bitcast.21), channel_id=1, source_target_pairs={{0,9},{1,8},{2,11},{3,10},{4,13},{5,12},{6,15},{7,14},{8,1},{9,0},... | collective-permute-start | bytes 49160 | tf_op jit(solution)/shard_map/ppermute | solution.py:164
  8.9 5.1 %collective-permute-start.5 = (f32[4,32,128]{2,1,0:T(8,128)S(1)}, f32[4,32,128]{2,1,0:T(8,128)S(1)}, u32[]{:S(2)}, u32[]{:S(2)}) collective-permute-start(f32[4,32,128]{2,1,0:T(8,128)S(1)} %pad_maximum_fusion.refs_2_), channel_id=1, source_target_pairs={{0,7},{1,6},{2,5},{3,4},{4,3},{5,2},{6,1},{7,0},{8,15},{9,14},{10,... | collective-permute-start | bytes 196616 | tf_op jit(solution)/shard_map/ppermute | solution.py:164
  11.6 4.3 %collective-permute-start.4 = (f32[4,32,128]{2,1,0:T(8,128)S(1)}, f32[4,32,128]{2,1,0:T(8,128)S(1)}, u32[]{:S(2)}, u32[]{:S(2)}) collective-permute-start(f32[4,32,128]{2,1,0:T(8,128)S(1)} %pad_maximum_fusion.refs_2_), channel_id=1, source_target_pairs={{0,5},{1,4},{2,7},{3,6},{4,1},{5,0},{6,3},{7,2},{8,13},{9,12},{10,... | collective-permute-start | bytes 196616 | tf_op jit(solution)/shard_map/ppermute | solution.py:164
  11.6 4.3 %collective-permute-start.3 = (f32[4,32,128]{2,1,0:T(8,128)S(1)}, f32[4,32,128]{2,1,0:T(8,128)S(1)}, u32[]{:S(2)}, u32[]{:S(2)}) collective-permute-start(f32[4,32,128]{2,1,0:T(8,128)S(1)} %pad_maximum_fusion.refs_2_), channel_id=1, source_target_pairs={{0,3},{1,2},{2,1},{3,0},{4,7},{5,6},{6,5},{7,4},{8,11},{9,10},{10,... | collective-permute-start | bytes 196616 | tf_op jit(solution)/shard_map/ppermute | solution.py:164
  12.3 4.0 %collective-permute-start.6 = (f32[4,32,128]{2,1,0:T(8,128)S(1)}, f32[4,32,128]{2,1,0:T(8,128)S(1)}, u32[]{:S(2)}, u32[]{:S(2)}) collective-permute-start(f32[4,32,128]{2,1,0:T(8,128)S(1)} %pad_maximum_fusion.refs_2_), channel_id=1, source_target_pairs={{0,1},{1,0},{2,3},{3,2},{4,5},{5,4},{6,7},{7,6},{8,9},{9,8},{10,11... | collective-permute-start | bytes 196616 | tf_op jit(solution)/shard_map/ppermute | solution.py:164
  14.0 2.4 %collective-permute-start.9 = (f32[4,32,128]{2,1,0:T(8,128)S(1)}, f32[4,32,128]{2,1,0:T(8,128)S(1)}, u32[]{:S(2)}, u32[]{:S(2)}) collective-permute-start(f32[4,32,128]{2,1,0:T(8,128)S(1)} %collective-permute-done.5.refs_5_), channel_id=1, source_target_pairs={{0,1},{1,0},{2,3},{3,2},{4,5},{5,4},{6,7},{7,6},{8,9},{9,8},{10,11... | collective-permute-start | bytes 196616 | tf_op jit(solution)/shard_map/ppermute | solution.py:164
  15.8 1.3 %collective-permute-start.8 = (f32[4,32,128]{2,1,0:T(8,128)S(1)}, f32[4,32,128]{2,1,0:T(8,128)S(1)}, u32[]{:S(2)}, u32[]{:S(2)}) collective-permute-start(f32[4,32,128]{2,1,0:T(8,128)S(1)} %collective-permute-done.4.refs_4_), channel_id=1, source_target_pairs={{0,1},{1,0},{2,3},{3,2},{4,5},{5,4},{6,7},{7,6},{8,9},{9,8},{10,11... | collective-permute-start | bytes 196616 | tf_op jit(solution)/shard_map/ppermute | solution.py:164
  15.9 1.3 %collective-permute-start.7 = (f32[4,32,128]{2,1,0:T(8,128)S(1)}, f32[4,32,128]{2,1,0:T(8,128)S(1)}, u32[]{:S(2)}, u32[]{:S(2)}) collective-permute-start(f32[4,32,128]{2,1,0:T(8,128)S(1)} %collective-permute-done.3.refs_3_), channel_id=1, source_target_pairs={{0,1},{1,0},{2,3},{3,2},{4,5},{5,4},{6,7},{7,6},{8,9},{9,8},{10,11... | collective-permute-start | bytes 196616 | tf_op jit(solution)/shard_map/ppermute | solution.py:164
